TPU v7x, 512 devices: a whole 4x8x8 slice. The times are simulated.
512 devices in a mesh: fsdp: 16 (over x_hi, z), ctx: 32 (over x_lo, y, core).
Axes of the slice: x: 4 (x_hi: 2, x_lo: 2; x = x_hi * 2 + x_lo), y: 8, z: 8, core: 2. Of those that a mesh axis runs over, the one named last changes fastest.
Arguments:
- gate_value: bfloat16 [65536, 4096], P('ctx', 'fsdp'), may hold values from -6 to 6
- conv_input: bfloat16 [65536, 4096], P('ctx', 'fsdp'), may hold values from -6 to 6
- output_grad: bfloat16 [65536, 4096], P('ctx', 'fsdp'), may hold values from -6 to 6
- decay_rate: float32 [4096, 16], P(('fsdp', 'ctx')), may hold values from 1.5258789e-06 to 0.04
- residue: float32 [4096, 16], P(('fsdp', 'ctx')), may hold values from -0.3 to 0.3
Outputs:
- input_grad: bfloat16 [65536, 4096], P('ctx', 'fsdp')
- residue_grad: float32 [4096, 16], P(('fsdp', 'ctx'))
All inputs are finite; a program needn't handle non-finite values.
Results may differ from a plain program's by a relative error of at most 0.0049.
Values may be sent and summed in bfloat16 or wider, within the bound.
A program may use at most 64 MiB of HBM per device.

v0:
```python
import functools
import math

import jax
import jax.numpy as jnp
import numpy as np
from jax import lax
from jax.experimental import pallas as pl
from jax.experimental.pallas import tpu as pltpu
from jax.sharding import PartitionSpec as P

WIDTH = 32
TERMS = 8
CHUNKS = 8
CENTER = (WIDTH - 1) / 2
MESH = pl.DeviceIdType.MESH
f32 = jnp.float32
bf16 = jnp.bfloat16


def chebyshev(z):
    rows = [np.ones_like(z), z]
    while len(rows) < TERMS:
        rows.append(2 * z * rows[-1] - rows[-2])
    return np.stack(rows)


def tables():
    i = np.arange(WIDTH)
    basis = chebyshev((i - CENTER) / (WIDTH / 2))
    lag = i[None, :] - i[:, None]
    tri = np.where(lag >= 0, basis[:, np.maximum(lag, 0)], 0.0)
    size = CHUNKS * WIDTH
    inner = np.zeros((TERMS, size, size))
    moment = np.zeros((TERMS, CHUNKS, size))
    for j in range(CHUNKS):
        part = slice(j * WIDTH, (j + 1) * WIDTH)
        inner[:, part, part] = tri
        moment[:, j, part] = basis
    moment = moment.reshape(TERMS * CHUNKS, size)
    spread = np.concatenate([moment.T, moment.T], axis=1)
    return [np.asarray(a, np.float32).astype(jnp.bfloat16) for a in (inner, moment, spread)]


def shift_rows(v, by):
    rows = v.shape[0]
    return jnp.concatenate([v[by:], jnp.zeros((by, v.shape[1]), v.dtype)], axis=0)


def kernel(
    n, length,
    gate, xin, ograd, rate, resid, inner, moment, spread,
    out, rgrad,
    g_v, x_v, o_v, s_v, out_v, inner_v, moment_v, spread_v,
    pack, rates, m_s, n_s, gacc, tau, en, fx, fo, lam_s, a32_s, a256_s, lamh_s,
    sq, cin, p256, st, yin,
    sbuf, ntbuf, ubuf, rbuf, sgot, ntgot, ugot, rgot, rgt,
    in_sem, tab_sem, out_sem,
    rates_send, rates_recv, s_send, s_recv, nt_send, nt_recv, u_send, u_recv, r_send, r_recv,
):
    me = lax.axis_index("ctx")
    half, mode = me // 16, me % 16
    steps = g_v.shape[0]

    def others(body):
        def step(i, carry):
            body(lax.rem(me + i, n))
            return carry
        lax.fori_loop(1, n, step, 0)

    barrier = pltpu.get_barrier_semaphore()
    others(lambda e: pl.semaphore_signal(barrier, inc=1, device_id={"ctx": e}, device_id_type=MESH))

    tabs = [
        pltpu.make_async_copy(moment, moment_v, tab_sem.at[0]),
        pltpu.make_async_copy(inner, inner_v, tab_sem.at[1]),
        pltpu.make_async_copy(spread, spread_v, tab_sem.at[2]),
    ]

    def fetch(q):
        return [
            pltpu.make_async_copy(src.at[:, q], dst.at[q], in_sem.at[k, q])
            for k, (src, dst) in enumerate(((gate, g_v), (ograd, o_v), (xin, x_v)))
        ]

    tabs[0].start()
    for c in fetch(0):
        c.start()
    tabs[1].start()
    for q in range(1, steps):
        for c in fetch(q):
            c.start()
    tabs[2].start()

    pack[:, 0:16] = rate[...]
    pack[:, 16:32] = resid[...]
    mine = pl.ds(pl.multiple_of(me * 8, 8), 8)
    rates[mine] = pack[...]
    pl.semaphore_wait(barrier, n - 1)

    def send_rates(e):
        pltpu.make_async_remote_copy(
            pack, rates.at[mine], rates_send, rates_recv, device_id={"ctx": e}, device_id_type=MESH
        ).start()

    others(send_rates)

    for k in range(TERMS):
        gacc[k] = jnp.zeros_like(gacc[k])
    tabs[0].wait()
    tabs[1].wait()

    def first(q, carry):
        for c in fetch(q):
            c.wait()
        s = (o_v[q].astype(f32) * g_v[q].astype(f32)).astype(bf16).reshape(256, 256)
        x = x_v[q].reshape(256, 256)
        s_v[q] = s
        m_s[q] = jnp.dot(moment_v[...], s, preferred_element_type=f32)
        n_s[q] = jnp.dot(moment_v[...], x, preferred_element_type=f32)
        wide = x.astype(f32)
        for k in range(TERMS):
            near = jnp.dot(inner_v[k], s, preferred_element_type=f32)
            gacc[k] += jnp.sum((near * wide).reshape(32, 8, 256), axis=0)
        return carry

    lax.fori_loop(0, steps, first, 0)

    pltpu.make_async_copy(rates.at[pl.ds(0, 8 * (n - 1))], rates.at[pl.ds(0, 8 * (n - 1))], rates_recv).wait()
    turned = rates[...].T
    lam, res = turned[0:16], turned[16:32]
    lam_s[...] = lam
    lamh_s[0:16] = lam[:, 0:128]
    lamh_s[16:32] = lam[:, 128:256]
    a32_s[...] = jnp.exp(-WIDTH * lam)
    a256_s[...] = jnp.exp(-(WIDTH * steps) * lam)
    ahead = jnp.exp(-CENTER * lam)
    behind = jnp.exp(-(WIDTH - CENTER) * lam)
    h = lam * (WIDTH / 4)
    w = h * h
    power = jnp.ones_like(h)
    for k in range(TERMS):
        tail = 1.0 + w * (1.0 / (4 * (k + 4)))
        for m in (3, 2, 1):
            tail = 1.0 + w * tail * (1.0 / (m * (k + m)))
        term = power * tail * ((1.0 if k == 0 else 2.0) / math.factorial(k))
        e = ahead * (term if k % 2 == 0 else -term)
        b = behind * term
        en[k] = e
        fx[k] = b
        fo[k] = b * res
        tau[k] = jnp.sum(e * res, axis=0, keepdims=True)
        power = power * h

    def scan(r, carry):
        row = pl.ds(r, 1)
        e = [en[k, row, :] for k in range(TERMS)]
        a = a32_s[row, :]
        u = None
        for q in reversed(range(steps)):
            new = e[0] * m_s[q, 0:8]
            for k in range(1, TERMS):
                new = new + e[k] * m_s[q, 8 * k : 8 * k + 8]
            sq[q, r] = new
            u = new if u is None else new + a * u
        big = a256_s[row, :]
        for by in (1, 2, 4):
            u = u + big * shift_rows(u, by)
            big = big * big
        sbuf[r] = u[0:1, 0:128]
        sbuf[16 + r] = u[0:1, 128:256]
        cin[r] = shift_rows(u, 1)
        return carry

    lax.fori_loop(0, 16, scan, 0)
    sgot[me] = sbuf[me]

    def send_rows(src, dst, send, recv):
        def body(e):
            pltpu.make_async_remote_copy(
                src.at[e], dst.at[me], send, recv, device_id={"ctx": e}, device_id_type=MESH
            ).start()
        return body

    def arrived(ref, sem):
        view = ref.at[pl.ds(0, n - 1)]
        pltpu.make_async_copy(view, view, sem).wait()

    others(send_rows(sbuf, sgot, s_send, s_recv))

    behind_chunks = (7 - lax.broadcasted_iota(jnp.int32, (8, 256), 0)).astype(f32) * (-float(WIDTH * steps))
    gsum = [jnp.sum(gacc[k], axis=0, keepdims=True) for k in range(TERMS)]

    def share(r, carry):
        row = pl.ds(r, 1)
        f = [fx[k, row, :] for k in range(TERMS)]
        a = a32_s[row, :]
        reach = jnp.exp(behind_chunks * lam_s[row, :])
        p256[r] = reach
        u = cin[r]
        acc = jnp.zeros((8, 256), f32)
        tail = jnp.zeros((8, 256), f32)
        fall = jnp.ones((1, 256), f32)
        for q in reversed(range(steps)):
            v = f[0] * n_s[q, 0:8]
            for k in range(1, TERMS):
                v = v + f[k] * n_s[q, 8 * k : 8 * k + 8]
            acc = acc + v * u
            tail = tail + v * fall
            if q:
                u = sq[q, r] + a * u
                fall = fall * a
        near = jnp.sum(acc, axis=0, keepdims=True)
        for k in range(TERMS):
            near = near + en[k, row, :] * gsum[k]
        tail = jnp.sum(tail * reach, axis=0, keepdims=True)
        ntbuf[r, 0:1] = near[:, 0:128]
        ntbuf[16 + r, 0:1] = near[:, 128:256]
        ntbuf[r, 1:2] = tail[:, 0:128]
        ntbuf[16 + r, 1:2] = tail[:, 128:256]
        return carry

    lax.fori_loop(0, 16, share, 0)
    ntgot[me] = ntbuf[me]
    others(send_rows(ntbuf, ntgot, nt_send, nt_recv))

    arrived(sgot, s_recv)
    v = sgot[:, 0, :]
    big = jnp.exp(lamh_s[pl.ds(me, 1), :] * (-float(WIDTH * steps * CHUNKS)))
    for by in (1, 2, 4, 8, 16):
        v = v + big * shift_rows(v, by)
        big = big * big
    v = shift_rows(v, 1)
    ubuf[:, 0, :] = v
    ugot[me] = ubuf[me]
    others(send_rows(ubuf, ugot, u_send, u_recv))

    arrived(ntgot, nt_recv)
    total = jnp.sum(ntgot[:, 0, :] + ntgot[:, 1, :] * v, axis=0, keepdims=True) * (1.0 / length)
    rbuf[...] = total
    rgot[mode] = total

    def send_total(i, carry):
        e = half * 16 + lax.rem(mode + i, 16)
        pltpu.make_async_remote_copy(
            rbuf, rgot.at[mode], r_send, r_recv, device_id={"ctx": e}, device_id_type=MESH
        ).start()
        return carry

    lax.fori_loop(1, 16, send_total, 0)

    def within(q, carry):
        s = s_v[q]
        acc = tau[0] * jnp.dot(inner_v[0], s, preferred_element_type=f32)
        for k in range(1, TERMS):
            acc = acc + tau[k] * jnp.dot(inner_v[k], s, preferred_element_type=f32)
        yin[q] = acc
        return carry

    lax.fori_loop(0, steps, within, 0)
    tabs[2].wait()

    arrived(ugot, u_recv)
    for r in range(16):
        u = jnp.concatenate([ugot[r], ugot[16 + r]], axis=1)
        st[r] = cin[r] + p256[r] * u

    def emit(q):
        return pltpu.make_async_copy(out_v.at[q], out.at[:, q], out_sem.at[q])

    def last(i, carry):
        q = steps - 1 - i
        levels = [jnp.zeros((8, 256), f32)] * TERMS
        for r in range(16):
            u = st[r]
            for k in range(TERMS):
                levels[k] = levels[k] + fo[k, r : r + 1, :] * u
            st[r] = sq[q, r] + a32_s[r : r + 1, :] * u
        level = jnp.concatenate(levels, axis=0)
        high = level.astype(bf16)
        low = (level - high.astype(f32)).astype(bf16)
        both = jnp.concatenate([high, low], axis=0)
        y = yin[q] + jnp.dot(spread_v[...], both, preferred_element_type=f32)
        out_v[q] = y.astype(bf16).reshape(CHUNKS, WIDTH, 256)
        emit(q).start()
        return carry

    lax.fori_loop(0, steps, last, 0)

    view = rgot.at[pl.ds(0, 15)]
    pltpu.make_async_copy(view, view, r_recv).wait()
    rgt[:, 0:16] = rgot[:, 0, :].T
    rgrad[...] = rgt[pl.ds(pl.multiple_of(mode * 8, 8), 8), 0:16]

    view = rates.at[pl.ds(0, 8 * (n - 1))]
    pltpu.make_async_copy(view, view, rates_send).wait()
    arrived(sbuf, s_send)
    arrived(ntbuf, nt_send)
    arrived(ubuf, u_send)
    view = rgot.at[pl.ds(0, 15)]
    pltpu.make_async_copy(view, view, r_send).wait()
    for q in range(steps):
        emit(q).wait()


def local(inner, moment, spread, gate_value, conv_input, output_grad, decay_rate, residue):
    tokens, channels = gate_value.shape
    n = lax.axis_size("ctx")
    steps = tokens // (CHUNKS * WIDTH)
    cut = (CHUNKS, steps, WIDTH, channels)
    V = pltpu.VMEM
    dma = pltpu.SemaphoreType.DMA
    blocks = (steps, CHUNKS, WIDTH, channels)
    size = CHUNKS * WIDTH
    scratch = [
        V(blocks, bf16), V(blocks, bf16), V(blocks, bf16), V((steps, size, channels), bf16), V(blocks, bf16),
        V(inner.shape, bf16), V(moment.shape, bf16), V(spread.shape, bf16),
        V((8, 128), f32), V((8 * n, 128), f32),
        V((steps, TERMS * CHUNKS, channels), f32), V((steps, TERMS * CHUNKS, channels), f32),
        V((TERMS, 8, channels), f32), V((TERMS, 1, channels), f32),
        V((TERMS, 16, channels), f32), V((TERMS, 16, channels), f32), V((TERMS, 16, channels), f32),
        V((16, channels), f32), V((16, channels), f32), V((16, channels), f32), V((32, 128), f32),
        V((steps, 16, 8, channels), f32), V((16, 8, channels), f32), V((16, 8, channels), f32), V((16, 8, channels), f32),
        V((steps, size, channels), f32),
        V((n, 1, 128), f32), V((n, 2, 128), f32), V((n, 1, 128), f32), V((1, 128), f32),
        V((n, 1, 128), f32), V((n, 2, 128), f32), V((n, 1, 128), f32), V((16, 1, 128), f32), V((128, 128), f32),
        dma((3, steps)), dma((3,)), dma((steps,)),
    ] + [dma] * 10
    vmem_spec = pl.BlockSpec(memory_space=pltpu.VMEM)
    any_spec = pl.BlockSpec(memory_space=pl.ANY)
    out, rgrad = pl.pallas_call(
        functools.partial(kernel, n, tokens * n),
        out_shape=(jax.ShapeDtypeStruct(cut, bf16), jax.ShapeDtypeStruct(residue.shape, f32)),
        in_specs=[any_spec] * 3 + [vmem_spec] * 2 + [any_spec] * 3,
        out_specs=(any_spec, vmem_spec),
        scratch_shapes=scratch,
        compiler_params=pltpu.CompilerParams(
            collective_id=0, has_side_effects=True, vmem_limit_bytes=48 * 1024 * 1024
        ),
    )(
        gate_value.reshape(cut), conv_input.reshape(cut), output_grad.reshape(cut),
        decay_rate, residue, inner, moment, spread,
    )
    return out.reshape(tokens, channels), rgrad


def solution(mesh):
    consts = tables()
    in_specs = (P(), P(), P()) + (P("ctx", "fsdp"),) * 3 + (P(("fsdp", "ctx"), None),) * 2
    out_specs = (P("ctx", "fsdp"), P(("fsdp", "ctx"), None))
    mapped = jax.shard_map(local, mesh=mesh, in_specs=in_specs, out_specs=out_specs, check_vma=False)

    def run(*args):
        return mapped(*[jnp.asarray(c) for c in consts], *args)

    return run
```

profile of v0, /device:TPU:1, one launch (start us, length us, event | category | flops | bytes accessed | tf_op | source)
XLA Modules:
  0.0 41.6 jit_solution(2190347667845887553)
XLA Ops:
  0.6 0.0 copy-start.6
  0.6 0.7 %copy-done.6 = f32[8,16]{1,0:T(8,128)S(1)} copy-done((f32[8,16]{1,0:T(8,128)S(1)}, f32[8,16]{1,0:T(8,128)}, u32[]{:S(2)}) %copy-start.6) | copy-done | bytes 536
  1.3 0.0 copy-start
  1.3 1.2 %copy-done = bf16[2048,256]{1,0:T(8,128)(2,1)S(1)} copy-done((bf16[2048,256]{1,0:T(8,128)(2,1)S(1)}, bf16[2048,256]{1,0:T(8,128)(2,1)}, u32[]{:S(2)}) %copy-start) | copy-done | bytes 1048600
  2.5 0.0 copy-start.1
  2.5 1.2 %copy-done.1 = bf16[2048,256]{1,0:T(8,128)(2,1)S(1)} copy-done((bf16[2048,256]{1,0:T(8,128)(2,1)S(1)}, bf16[2048,256]{1,0:T(8,128)(2,1)}, u32[]{:S(2)}) %copy-start.1) | copy-done | bytes 1048600
  3.8 0.0 copy-start.2
  3.8 1.2 %copy-done.2 = bf16[2048,256]{1,0:T(8,128)(2,1)S(1)} copy-done((bf16[2048,256]{1,0:T(8,128)(2,1)S(1)}, bf16[2048,256]{1,0:T(8,128)(2,1)}, u32[]{:S(2)}) %copy-start.2) | copy-done | bytes 1048600
  5.0 0.0 copy-start.3
  5.0 1.2 %copy-done.3 = bf16[8,256,256]{2,1,0:T(8,128)(2,1)S(1)} copy-done((bf16[8,256,256]{2,1,0:T(8,128)(2,1)S(1)}, bf16[8,256,256]{2,1,0:T(8,128)(2,1)}, u32[]{:S(2)}) %copy-start.3) | copy-done | bytes 1048600
  6.2 0.0 copy-start.4
  6.2 0.8 %copy-done.4 = bf16[256,128]{1,0:T(8,128)(2,1)S(1)} copy-done((bf16[256,128]{1,0:T(8,128)(2,1)S(1)}, bf16[256,128]{1,0:T(8,128)(2,1)}, u32[]{:S(2)}) %copy-start.4) | copy-done | bytes 65560
  7.1 0.0 copy-start.5
  7.1 0.8 %copy-done.5 = bf16[64,256]{1,0:T(8,128)(2,1)S(1)} copy-done((bf16[64,256]{1,0:T(8,128)(2,1)S(1)}, bf16[64,256]{1,0:T(8,128)(2,1)}, u32[]{:S(2)}) %copy-start.5) | copy-done | bytes 32792
  7.8 0.0 copy-start.7
  7.8 0.7 %copy-done.7 = f32[8,16]{1,0:T(8,128)S(1)} copy-done((f32[8,16]{1,0:T(8,128)S(1)}, f32[8,16]{1,0:T(8,128)}, u32[]{:S(2)}) %copy-start.7) | copy-done | bytes 536
  8.5 31.5 %shard_map.95 = (bf16[8,8,32,256]{3,2,1,0:T(8,128)(2,1)S(1)}, f32[8,16]{1,0:T(8,128)S(1)}) custom-call(bf16[8,8,32,256]{3,2,1,0:T(8,128)(2,1)S(1)} %bitcast.5, bf16[8,8,32,256]{3,2,1,0:T(8,128)(2,1)S(1)} %bitcast.6, bf16[8,8,32,256]{3,2,1,0:T(8,128)(2,1)S(1)} %bitcast.7, f32[8,16]{1,0:T(8,128)S(1)} %copy-done.6, f32[8,16]{1,0:T(8,128)S(1)} %copy-done.7, ...), custom_call_target="tpu_custom_call" | custom-call | tf_op jit(solution)/shard_map/pallas_call | solution.py:331
  40.0 1.0 %copy.12 = bf16[2048,256]{1,0:T(8,128)(2,1)} copy(bf16[2048,256]{1,0:T(8,128)(2,1)S(1)} %bitcast.4) | data formatting | bytes 2097152
  41.0 0.6 %copy.13 = f32[8,16]{1,0:T(8,128)} copy(f32[8,16]{1,0:T(8,128)S(1)} %get-tuple-element.9) | data formatting | bytes 1024
Async XLA Ops:
  0.6 0.7 %copy-start.6 = (f32[8,16]{1,0:T(8,128)S(1)}, f32[8,16]{1,0:T(8,128)}, u32[]{:S(2)}) copy-start(f32[8,16]{1,0:T(8,128)} %rate.1) | copy-start | bytes 1540
  1.3 1.2 %copy-start = (bf16[2048,256]{1,0:T(8,128)(2,1)S(1)}, bf16[2048,256]{1,0:T(8,128)(2,1)}, u32[]{:S(2)}) copy-start(bf16[2048,256]{1,0:T(8,128)(2,1)} %param.8) | copy-start | bytes 3145732
  2.5 1.2 %copy-start.1 = (bf16[2048,256]{1,0:T(8,128)(2,1)S(1)}, bf16[2048,256]{1,0:T(8,128)(2,1)}, u32[]{:S(2)}) copy-start(bf16[2048,256]{1,0:T(8,128)(2,1)} %param.9) | copy-start | bytes 3145732
  3.8 1.2 %copy-start.2 = (bf16[2048,256]{1,0:T(8,128)(2,1)S(1)}, bf16[2048,256]{1,0:T(8,128)(2,1)}, u32[]{:S(2)}) copy-start(bf16[2048,256]{1,0:T(8,128)(2,1)} %param.10) | copy-start | bytes 3145732
  5.0 1.2 %copy-start.3 = (bf16[8,256,256]{2,1,0:T(8,128)(2,1)S(1)}, bf16[8,256,256]{2,1,0:T(8,128)(2,1)}, u32[]{:S(2)}) copy-start(bf16[8,256,256]{2,1,0:T(8,128)(2,1)} %constant.6.clone.inner) | copy-start | bytes 3145732
  6.2 0.8 %copy-start.4 = (bf16[256,128]{1,0:T(8,128)(2,1)S(1)}, bf16[256,128]{1,0:T(8,128)(2,1)}, u32[]{:S(2)}) copy-start(bf16[256,128]{1,0:T(8,128)(2,1)} %constant.8.clone.spread) | copy-start | bytes 196612
  7.1 0.8 %copy-start.5 = (bf16[64,256]{1,0:T(8,128)(2,1)S(1)}, bf16[64,256]{1,0:T(8,128)(2,1)}, u32[]{:S(2)}) copy-start(bf16[64,256]{1,0:T(8,128)(2,1)} %constant.7.clone.moment) | copy-start | bytes 98308
  7.8 0.7 %copy-start.7 = (f32[8,16]{1,0:T(8,128)S(1)}, f32[8,16]{1,0:T(8,128)}, u32[]{:S(2)}) copy-start(f32[8,16]{1,0:T(8,128)} %resid.1) | copy-start | bytes 1540
where the time goes:
time: 42 us; the launch traced here: 41.6 us
  Pallas kernels  31.5 us (75%)
  local copies, waits for them, and re-layouts  9.42 us (22%)
  between operations  0.66 us (2%)
    pallas_call x1, Pallas kernels, local(): pl.pallas_call(functools.partial(kernel, n, tokens * n), out_shape=(jax.S...  31.5 us
    unnamed x18, local copies, waits for them, and re-layouts  9.42 us

commit v1 on v0

--- a/solution.py
+++ b/solution.py
@@ -51,11 +51,11 @@
     n, length,
     gate, xin, ograd, rate, resid, inner, moment, spread,
     out, rgrad,
-    g_v, x_v, o_v, s_v, out_v, inner_v, moment_v, spread_v,
+    g_v, x_v, o_v, s_v, inner_v, moment_v, spread_v, rate_v, resid_v,
     pack, rates, m_s, n_s, gacc, tau, en, fx, fo, lam_s, a32_s, a256_s, lamh_s,
     sq, cin, p256, st, yin,
     sbuf, ntbuf, ubuf, rbuf, sgot, ntgot, ugot, rgot, rgt,
-    in_sem, tab_sem, out_sem,
+    in_sem, tab_sem, par_sem,
     rates_send, rates_recv, s_send, s_recv, nt_send, nt_recv, u_send, u_recv, r_send, r_recv,
 ):
     me = lax.axis_index("ctx")
@@ -71,6 +71,9 @@
     barrier = pltpu.get_barrier_semaphore()
     others(lambda e: pl.semaphore_signal(barrier, inc=1, device_id={"ctx": e}, device_id_type=MESH))
 
+    par = [pltpu.make_async_copy(rate, rate_v, par_sem.at[0]), pltpu.make_async_copy(resid, resid_v, par_sem.at[1])]
+    for c in par:
+        c.start()
     tabs = [
         pltpu.make_async_copy(moment, moment_v, tab_sem.at[0]),
         pltpu.make_async_copy(inner, inner_v, tab_sem.at[1]),
@@ -92,8 +95,10 @@
             c.start()
     tabs[2].start()
 
-    pack[:, 0:16] = rate[...]
-    pack[:, 16:32] = resid[...]
+    for c in par:
+        c.wait()
+    pack[:, 0:16] = rate_v[...]
+    pack[:, 16:32] = resid_v[...]
     mine = pl.ds(pl.multiple_of(me * 8, 8), 8)
     rates[mine] = pack[...]
     pl.semaphore_wait(barrier, n - 1)
@@ -265,11 +270,7 @@
         u = jnp.concatenate([ugot[r], ugot[16 + r]], axis=1)
         st[r] = cin[r] + p256[r] * u
 
-    def emit(q):
-        return pltpu.make_async_copy(out_v.at[q], out.at[:, q], out_sem.at[q])
-
-    def last(i, carry):
-        q = steps - 1 - i
+    for q in reversed(range(steps)):
         levels = [jnp.zeros((8, 256), f32)] * TERMS
         for r in range(16):
             u = st[r]
@@ -281,11 +282,7 @@
         low = (level - high.astype(f32)).astype(bf16)
         both = jnp.concatenate([high, low], axis=0)
         y = yin[q] + jnp.dot(spread_v[...], both, preferred_element_type=f32)
-        out_v[q] = y.astype(bf16).reshape(CHUNKS, WIDTH, 256)
-        emit(q).start()
-        return carry
-
-    lax.fori_loop(0, steps, last, 0)
+        out[:, q] = y.astype(bf16).reshape(CHUNKS, WIDTH, 256)
 
     view = rgot.at[pl.ds(0, 15)]
     pltpu.make_async_copy(view, view, r_recv).wait()
@@ -299,8 +296,6 @@
     arrived(ubuf, u_send)
     view = rgot.at[pl.ds(0, 15)]
     pltpu.make_async_copy(view, view, r_send).wait()
-    for q in range(steps):
-        emit(q).wait()
 
 
 def local(inner, moment, spread, gate_value, conv_input, output_grad, decay_rate, residue):
@@ -313,8 +308,8 @@
     blocks = (steps, CHUNKS, WIDTH, channels)
     size = CHUNKS * WIDTH
     scratch = [
-        V(blocks, bf16), V(blocks, bf16), V(blocks, bf16), V((steps, size, channels), bf16), V(blocks, bf16),
-        V(inner.shape, bf16), V(moment.shape, bf16), V(spread.shape, bf16),
+        V(blocks, bf16), V(blocks, bf16), V(blocks, bf16), V((steps, size, channels), bf16),
+        V(inner.shape, bf16), V(moment.shape, bf16), V(spread.shape, bf16), V((8, 16), f32), V((8, 16), f32),
         V((8, 128), f32), V((8 * n, 128), f32),
         V((steps, TERMS * CHUNKS, channels), f32), V((steps, TERMS * CHUNKS, channels), f32),
         V((TERMS, 8, channels), f32), V((TERMS, 1, channels), f32),
@@ -324,23 +319,26 @@
         V((steps, size, channels), f32),
         V((n, 1, 128), f32), V((n, 2, 128), f32), V((n, 1, 128), f32), V((1, 128), f32),
         V((n, 1, 128), f32), V((n, 2, 128), f32), V((n, 1, 128), f32), V((16, 1, 128), f32), V((128, 128), f32),
-        dma((3, steps)), dma((3,)), dma((steps,)),
+        dma((3, steps)), dma((3,)), dma((2,)),
     ] + [dma] * 10
     vmem_spec = pl.BlockSpec(memory_space=pltpu.VMEM)
-    any_spec = pl.BlockSpec(memory_space=pl.ANY)
+    hbm_spec = pl.BlockSpec(memory_space=pltpu.HBM)
     out, rgrad = pl.pallas_call(
         functools.partial(kernel, n, tokens * n),
         out_shape=(jax.ShapeDtypeStruct(cut, bf16), jax.ShapeDtypeStruct(residue.shape, f32)),
-        in_specs=[any_spec] * 3 + [vmem_spec] * 2 + [any_spec] * 3,
-        out_specs=(any_spec, vmem_spec),
+        in_specs=[hbm_spec] * 8,
+        out_specs=(vmem_spec, vmem_spec),
         scratch_shapes=scratch,
         compiler_params=pltpu.CompilerParams(
-            collective_id=0, has_side_effects=True, vmem_limit_bytes=48 * 1024 * 1024
+            collective_id=0, has_side_effects=True, vmem_limit_bytes=24 * 1024 * 1024
         ),
-    )(
-        gate_value.reshape(cut), conv_input.reshape(cut), output_grad.reshape(cut),
-        decay_rate, residue, inner, moment, spread,
-    )
+    )(*[
+        pltpu.with_memory_space_constraint(a, pltpu.HBM)
+        for a in (
+            gate_value.reshape(cut), conv_input.reshape(cut), output_grad.reshape(cut),
+            decay_rate, residue, inner, moment, spread,
+        )
+    ])
     return out.reshape(tokens, channels), rgrad
 
 

time: 42 us -> 32.7 us (0.78)
  local copies, waits for them, and re-layouts: 9.42 us -> 1.56 us
  Pallas kernels: 31.5 us -> 30.4 us
    unnamed x18 -> x2, local copies, waits for them, and re-layouts: 9.42 us -> 1.56 us
    pallas_call x1, Pallas kernels: 31.5 us -> 30.4 us  [local(): pl.pallas_call(functools.partial(kernel, n, tokens * n), out_shape=(jax.S...]
where the time goes in v1:
time: 32.7 us; the launch traced here: 32.6 us
  Pallas kernels  30.4 us (93%)
  local copies, waits for them, and re-layouts  1.56 us (5%)
  between operations  0.64 us (2%)
    pallas_call x1, Pallas kernels, local(): pl.pallas_call(functools.partial(kernel, n, tokens * n), out_shape=(jax.S...  30.4 us
    unnamed x2, local copies, waits for them, and re-layouts  1.56 us

profile of v1, /device:TPU:1, one launch (start us, length us, event | category | flops | bytes accessed | tf_op | source)
XLA Modules:
  0.0 32.6 jit_solution(6349698122934696754)
XLA Ops:
  0.6 30.4 %shard_map.95 = (bf16[8,8,32,256]{3,2,1,0:T(8,128)(2,1)S(1)}, f32[8,16]{1,0:T(8,128)S(1)}) custom-call(bf16[8,8,32,256]{3,2,1,0:T(8,128)(2,1)} %bitcast.5, bf16[8,8,32,256]{3,2,1,0:T(8,128)(2,1)} %bitcast.6, bf16[8,8,32,256]{3,2,1,0:T(8,128)(2,1)} %bitcast.7, f32[8,16]{1,0:T(8,128)} %rate.1, f32[8,16]{1,0:T(8,128)} %resid.1, ...), custom_call_target="tpu_custom_call" | custom-call | tf_op jit(solution)/shard_map/pallas_call | solution.py:326
  31.0 1.0 %copy.12 = bf16[2048,256]{1,0:T(8,128)(2,1)} copy(bf16[2048,256]{1,0:T(8,128)(2,1)S(1)} %bitcast.4) | data formatting | bytes 2097152
  32.0 0.6 %copy.13 = f32[8,16]{1,0:T(8,128)} copy(f32[8,16]{1,0:T(8,128)S(1)} %get-tuple-element.9) | data formatting | bytes 1024

commit v2 on v1

v2 whole, which is shorter than its diff:
```python
import functools
import math

import jax
import jax.numpy as jnp
import numpy as np
from jax import lax
from jax.experimental import pallas as pl
from jax.experimental.pallas import tpu as pltpu
from jax.sharding import PartitionSpec as P

WIDTH = 32
TERMS = 8
CHUNKS = 8
CENTER = (WIDTH - 1) / 2
POINTS = 48
MESH = pl.DeviceIdType.MESH
f32 = jnp.float32
bf16 = jnp.bfloat16


def chebyshev(z):
    rows = [np.ones_like(z), z]
    while len(rows) < TERMS:
        rows.append(2 * z * rows[-1] - rows[-2])
    return np.stack(rows)


def tables(steps):
    i = np.arange(WIDTH)
    basis = chebyshev((i - CENTER) / (WIDTH / 2))
    lag = i[None, :] - i[:, None]
    tri = np.where(lag >= 0, basis[:, np.maximum(lag, 0)], 0.0)
    size = CHUNKS * WIDTH
    inner = np.zeros((TERMS, size, size))
    moment = np.zeros((TERMS, CHUNKS, size))
    for j in range(CHUNKS):
        part = slice(j * WIDTH, (j + 1) * WIDTH)
        inner[:, part, part] = tri
        moment[:, j, part] = basis
    moment = moment.reshape(TERMS * CHUNKS, size)
    spread = np.concatenate([moment.T, moment.T], axis=1)

    total = steps * size
    angle = (2 * np.arange(POINTS) + 1) * math.pi / (2 * POINTS)
    points = (total - 1) / 2 + total / 2 * np.cos(angle)
    order = np.arange(POINTS)
    z = (np.arange(total) - (total - 1) / 2) / (total / 2)
    weight = np.where(order == 0, 1.0, 2.0) / POINTS
    basis = np.cos(np.outer(angle, order)) * weight @ np.cos(np.outer(order, np.arccos(z)))
    basis = basis.reshape(POINTS, CHUNKS, steps, WIDTH).transpose(2, 0, 1, 3).reshape(steps, POINTS, size)
    high = basis.astype(np.float32).astype(jnp.bfloat16)
    low = (basis - high.astype(np.float64)).astype(np.float32).astype(jnp.bfloat16)
    whole = np.concatenate([high, low], axis=1)
    points = np.broadcast_to(points[:, None], (POINTS, 128)).astype(np.float32)
    return [np.asarray(a, np.float32).astype(jnp.bfloat16) for a in (inner, moment, spread)] + [whole, points]


def shift_rows(v, by):
    rows = v.shape[0]
    return jnp.concatenate([v[by:], jnp.zeros((by, v.shape[1]), v.dtype)], axis=0)


def kernel(
    n, length,
    gate, xin, ograd, rate, resid, inner, moment, spread, whole, points,
    out, rgrad,
    g_v, x_v, o_v, s_v, inner_v, moment_v, spread_v, whole_v, points_v, rate_v, resid_v,
    own, pack, rates, m_s, n_s, gacc, tau, en, fx, fo, lam_s, a32_s, a256_s, lamh_s,
    sq, cin, p256, st, yin, stack,
    table, mbuf, mgot, ubuf, ugot, rbuf, rgot,
    in_sem, tab_sem, par_sem,
    rates_send, rates_recv, m_send, m_recv, u_send, u_recv, r_send, r_recv,
):
    me = lax.axis_index("ctx")
    steps = g_v.shape[0]
    chunk = WIDTH * steps
    span = chunk * CHUNKS

    def others(body):
        def step(i, carry):
            body(lax.rem(me + i, n))
            return carry
        lax.fori_loop(1, n, step, 0)

    def put(src, dst, send, recv, e):
        pltpu.make_async_remote_copy(src, dst, send, recv, device_id={"ctx": e}, device_id_type=MESH).start()

    def arrived(view, sem):
        pltpu.make_async_copy(view, view, sem).wait()

    barrier = pltpu.get_barrier_semaphore()
    others(lambda e: pl.semaphore_signal(barrier, inc=1, device_id={"ctx": e}, device_id_type=MESH))

    par = [pltpu.make_async_copy(rate, rate_v, par_sem.at[0]), pltpu.make_async_copy(resid, resid_v, par_sem.at[1])]
    for c in par:
        c.start()
    tabs = [
        pltpu.make_async_copy(src, dst, tab_sem.at[k])
        for k, (src, dst) in enumerate((
            (whole, whole_v), (points, points_v), (moment, moment_v), (inner, inner_v), (spread, spread_v)
        ))
    ]

    arrays = ((gate, g_v), (ograd, o_v), (xin, x_v))

    def fetch(q, which):
        return [
            pltpu.make_async_copy(arrays[k][0].at[:, q], arrays[k][1].at[q], in_sem.at[k, q]) for k in which
        ]

    for c in fetch(0, (0, 1)):
        c.start()
    tabs[0].start()
    for q in range(1, steps):
        for c in fetch(q, (0, 1)):
            c.start()
    for c in tabs[1:4]:
        c.start()
    for q in range(steps):
        fetch(q, (2,))[0].start()
    tabs[4].start()

    own[...] = jnp.zeros_like(own)
    stack[...] = jnp.zeros_like(stack)
    for c in par:
        c.wait()
    own[0, :, 0:16] = rate_v[...]
    own[1, :, 0:16] = resid_v[...]
    for i in range(2):
        row = own[i, 0:1]
        for c in range(1, 8):
            row = row + pltpu.roll(own[i, c : c + 1], 128 - 16 * c, 1)
        pack[i : i + 1] = row
    row = own[0, 0:1]
    for c in range(1, 8):
        row = row + pltpu.roll(own[0, c : c + 1], 16 * c, 1)
    rates[me] = pack[...]

    lane = lax.broadcasted_iota(jnp.int32, (8, 128), 1)
    group, place = lane // 16, lax.broadcasted_iota(jnp.int32, (8, 128), 0)

    def to_rows(block, count, dst):
        turned = block.T
        for e in range(n):
            tile = pltpu.roll(turned[8 * e : 8 * e + 8], 0, 1, stride=16, stride_axis=0)
            for i in range(count):
                line = jnp.sum(jnp.where(group == (place + i) % 8, tile, 0.0), axis=0, keepdims=True)
                dst[e, i : i + 1] = line if i == 0 else pltpu.roll(line, 128 - 16 * i, 1)

    tabs[0].wait()
    for q in range(steps):
        for c in fetch(q, (0, 1)):
            c.wait()
        s = (o_v[q].astype(f32) * g_v[q].astype(f32)).astype(bf16).reshape(256, 256)
        s_v[q] = s
        part = jnp.dot(whole_v[q], s, preferred_element_type=f32)
        sums = part if q == 0 else sums + part
    stack[0:POINTS] = sums[0:POINTS] + sums[POINTS:]
    to_rows(stack[...], POINTS // 16, mbuf)
    mgot[me] = mbuf[me]

    tabs[1].wait()
    falls = jnp.exp(points_v[...] * (-row))
    square = (128, 128)
    same = lax.broadcasted_iota(jnp.int32, square, 0) // 16 == lax.broadcasted_iota(jnp.int32, square, 1) // 16
    for i in range(POINTS // 16):
        part = jnp.concatenate([falls[16 * i : 16 * i + 16]] * 8, axis=0)
        table[128 * i : 128 * i + 128] = jnp.where(same, part, 0.0)

    pl.semaphore_wait(barrier, n - 1)
    others(lambda e: put(mbuf.at[e], mgot.at[me], m_send, m_recv, e))
    others(lambda e: put(pack, rates.at[me], rates_send, rates_recv, e))

    for k in range(TERMS):
        gacc[k] = jnp.zeros_like(gacc[k])
    tabs[2].wait()
    tabs[3].wait()

    def first(q, carry):
        fetch(q, (2,))[0].wait()
        s = s_v[q]
        x = x_v[q].reshape(256, 256)
        m_s[q] = jnp.dot(moment_v[...], s, preferred_element_type=f32)
        n_s[q] = jnp.dot(moment_v[...], x, preferred_element_type=f32)
        wide = x.astype(f32)
        for k in range(TERMS):
            near = jnp.dot(inner_v[k], s, preferred_element_type=f32)
            gacc[k] += jnp.sum((near * wide).reshape(32, 8, 256), axis=0)
        return carry

    lax.fori_loop(0, steps, first, 0)

    arrived(mgot.at[pl.ds(0, n - 1)], m_recv)
    sums = jnp.concatenate([mgot[:, i, :] for i in range(POINTS // 16)], axis=1)
    v = jnp.dot(sums, table[...], precision=lax.Precision.HIGHEST, preferred_element_type=f32)
    big = jnp.exp(row * (-float(span)))
    for by in (1, 2, 4, 8, 16):
        v = v + big * shift_rows(v, by)
        big = big * big
    states = shift_rows(v, 1)
    wide_group = lax.broadcasted_iota(jnp.int32, (n, 128), 1) // 16
    mirrored = states
    for c in range(1, 8):
        mirrored = jnp.where(wide_group == 8 - c, pltpu.roll(states, (128 - 32 * c) % 128, 1), mirrored)
    ubuf[:, 0, :] = mirrored
    ugot[me] = ubuf[me]
    others(lambda e: put(ubuf.at[e], ugot.at[me], u_send, u_recv, e))

    arrived(rates.at[pl.ds(0, n - 1)], rates_recv)
    tiles = []
    for e in range(n):
        a = pltpu.roll(jnp.broadcast_to(rates[e, 0:1], (8, 128)), 0, 1, stride=16, stride_axis=0)
        b = pltpu.roll(jnp.broadcast_to(rates[e, 1:2], (8, 128)), 16, 1, stride=16, stride_axis=0)
        tiles.append(jnp.where(lane < 16, a, b))
    turned = jnp.concatenate(tiles, axis=0).T
    lam, res = turned[0:16], turned[16:32]
    lam_s[...] = lam
    lamh_s[0:16] = lam[:, 0:128]
    lamh_s[16:32] = lam[:, 128:256]
    a32_s[...] = jnp.exp(-WIDTH * lam)
    a256_s[...] = jnp.exp(-chunk * lam)
    ahead = jnp.exp(-CENTER * lam)
    behind = jnp.exp(-(WIDTH - CENTER) * lam)
    h = lam * (WIDTH / 4)
    w = h * h
    power = jnp.ones_like(h)
    for k in range(TERMS):
        tail = 1.0 + w * (1.0 / (4 * (k + 4)))
        for m in (3, 2, 1):
            tail = 1.0 + w * tail * (1.0 / (m * (k + m)))
        term = power * tail * ((1.0 if k == 0 else 2.0) / math.factorial(k))
        e = ahead * (term if k % 2 == 0 else -term)
        b = behind * term
        en[k] = e
        fx[k] = b
        fo[k] = b * res
        tau[k] = jnp.sum(e * res, axis=0, keepdims=True)
        power = power * h

    def scan(r, carry):
        row = pl.ds(r, 1)
        e = [en[k, row, :] for k in range(TERMS)]
        a = a32_s[row, :]
        u = None
        for q in reversed(range(steps)):
            new = e[0] * m_s[q, 0:8]
            for k in range(1, TERMS):
                new = new + e[k] * m_s[q, 8 * k : 8 * k + 8]
            sq[q, r] = new
            u = new if u is None else new + a * u
        big = a256_s[row, :]
        for by in (1, 2, 4):
            u = u + big * shift_rows(u, by)
            big = big * big
        cin[r] = shift_rows(u, 1)
        return carry

    lax.fori_loop(0, 16, scan, 0, unroll=2)

    behind_chunks = (7 - lax.broadcasted_iota(jnp.int32, (8, 256), 0)).astype(f32) * (-float(chunk))
    gsum = [jnp.sum(gacc[k], axis=0, keepdims=True) for k in range(TERMS)]

    def share(r, carry):
        row = pl.ds(r, 1)
        f = [fx[k, row, :] for k in range(TERMS)]
        a = a32_s[row, :]
        reach = jnp.exp(behind_chunks * lam_s[row, :])
        p256[r] = reach
        u = cin[r]
        acc = jnp.zeros((8, 256), f32)
        tail = jnp.zeros((8, 256), f32)
        fall = jnp.ones((1, 256), f32)
        for q in reversed(range(steps)):
            v = f[0] * n_s[q, 0:8]
            for k in range(1, TERMS):
                v = v + f[k] * n_s[q, 8 * k : 8 * k + 8]
            acc = acc + v * u
            tail = tail + v * fall
            if q:
                u = sq[q, r] + a * u
                fall = fall * a
        near = jnp.sum(acc, axis=0, keepdims=True)
        for k in range(TERMS):
            near = near + en[k, row, :] * gsum[k]
        stack[row] = near
        stack[pl.ds(16 + r, 1)] = jnp.sum(tail * reach, axis=0, keepdims=True)
        return carry

    lax.fori_loop(0, 16, share, 0, unroll=2)

    to_rows(stack[...], 2, rbuf)
    rgot[me] = rbuf[me]
    others(lambda e: put(rbuf.at[e], rgot.at[me], r_send, r_recv, e))

    def within(q, carry):
        s = s_v[q]
        acc = tau[0] * jnp.dot(inner_v[0], s, preferred_element_type=f32)
        for k in range(1, TERMS):
            acc = acc + tau[k] * jnp.dot(inner_v[k], s, preferred_element_type=f32)
        yin[q] = acc
        return carry

    lax.fori_loop(0, steps, within, 0)
    tabs[4].wait()

    arrived(ugot.at[pl.ds(0, n - 1)], u_recv)
    tiles = [
        pltpu.roll(jnp.broadcast_to(ugot[e], (8, 128)), 0, 1, stride=16, stride_axis=0) for e in range(n)
    ]
    turned = jnp.concatenate(tiles, axis=0).T
    for r in range(16):
        st[r] = cin[r] + p256[r] * turned[r : r + 1]

    for q in reversed(range(steps)):
        levels = [jnp.zeros((8, 256), f32)] * TERMS
        for r in range(16):
            u = st[r]
            for k in range(TERMS):
                levels[k] = levels[k] + fo[k, r : r + 1, :] * u
            if q:
                st[r] = sq[q, r] + a32_s[r : r + 1, :] * u
        level = jnp.concatenate(levels, axis=0)
        high = level.astype(bf16)
        low = (level - high.astype(f32)).astype(bf16)
        both = jnp.concatenate([high, low], axis=0)
        y = yin[q] + jnp.dot(spread_v[...], both, preferred_element_type=f32)
        out[:, q] = y.astype(bf16).reshape(CHUNKS, WIDTH, 256)

    arrived(rgot.at[pl.ds(0, n - 1)], r_recv)
    total = jnp.sum(rgot[:, 0, :] + rgot[:, 1, :] * states, axis=0, keepdims=True)
    total = total * (1.0 / length)
    for c in range(8):
        moved = total if c == 0 else pltpu.roll(total, 128 - 16 * c, 1)
        rgrad[c : c + 1] = moved[:, 0:16]

    arrived(rates.at[pl.ds(0, n - 1)], rates_send)
    arrived(mgot.at[pl.ds(0, n - 1)], m_send)
    arrived(ugot.at[pl.ds(0, n - 1)], u_send)
    arrived(rgot.at[pl.ds(0, n - 1)], r_send)


def local(inner, moment, spread, whole, points, gate_value, conv_input, output_grad, decay_rate, residue):
    tokens, channels = gate_value.shape
    n = lax.axis_size("ctx")
    steps = tokens // (CHUNKS * WIDTH)
    cut = (CHUNKS, steps, WIDTH, channels)
    V = pltpu.VMEM
    dma = pltpu.SemaphoreType.DMA
    blocks = (steps, CHUNKS, WIDTH, channels)
    size = CHUNKS * WIDTH
    scratch = [
        V(blocks, bf16), V(blocks, bf16), V(blocks, bf16), V((steps, size, channels), bf16),
        V(inner.shape, bf16), V(moment.shape, bf16), V(spread.shape, bf16), V(whole.shape, bf16), V(points.shape, f32), V((8, 16), f32), V((8, 16), f32),
        V((2, 8, 128), f32), V((2, 128), f32), V((n, 2, 128), f32),
        V((steps, TERMS * CHUNKS, channels), f32), V((steps, TERMS * CHUNKS, channels), f32),
        V((TERMS, 8, channels), f32), V((TERMS, 1, channels), f32),
        V((TERMS, 16, channels), f32), V((TERMS, 16, channels), f32), V((TERMS, 16, channels), f32),
        V((16, channels), f32), V((16, channels), f32), V((16, channels), f32), V((32, 128), f32),
        V((steps, 16, 8, channels), f32), V((16, 8, channels), f32), V((16, 8, channels), f32), V((16, 8, channels), f32),
        V((steps, size, channels), f32), V((128, channels), f32),
        V((8 * POINTS, 128), f32), V((n, POINTS // 16, 128), f32), V((n, POINTS // 16, 128), f32),
        V((n, 1, 128), f32), V((n, 1, 128), f32), V((n, 2, 128), f32), V((n, 2, 128), f32),
        dma((3, steps)), dma((5,)), dma((2,)),
    ] + [dma] * 8
    vmem_spec = pl.BlockSpec(memory_space=pltpu.VMEM)
    hbm_spec = pl.BlockSpec(memory_space=pltpu.HBM)
    out, rgrad = pl.pallas_call(
        functools.partial(kernel, n, tokens * n),
        out_shape=(jax.ShapeDtypeStruct(cut, bf16), jax.ShapeDtypeStruct(residue.shape, f32)),
        in_specs=[hbm_spec] * 10,
        out_specs=(vmem_spec, vmem_spec),
        scratch_shapes=scratch,
        compiler_params=pltpu.CompilerParams(
            collective_id=0, has_side_effects=True, vmem_limit_bytes=24 * 1024 * 1024
        ),
    )(*[
        pltpu.with_memory_space_constraint(a, pltpu.HBM)
        for a in (
            gate_value.reshape(cut), conv_input.reshape(cut), output_grad.reshape(cut),
            decay_rate, residue, inner, moment, spread, whole, points,
        )
    ])
    return out.reshape(tokens, channels), rgrad


def solution(mesh):
    consts = tables(8)
    in_specs = (P(),) * 5 + (P("ctx", "fsdp"),) * 3 + (P(("fsdp", "ctx"), None),) * 2
    out_specs = (P("ctx", "fsdp"), P(("fsdp", "ctx"), None))
    mapped = jax.shard_map(local, mesh=mesh, in_specs=in_specs, out_specs=out_specs, check_vma=False)

    def run(*args):
        return mapped(*[jnp.asarray(c) for c in consts], *args)

    return run
```

time: 32.7 us -> 27.6 us (0.84)
  Pallas kernels: 30.4 us -> 25.2 us
    pallas_call x1, Pallas kernels: 30.4 us -> 25.2 us  [local(): pl.pallas_call(functools.partial(kernel, n, tokens * n), out_shape=(jax.S...]
where the time goes in v2:
time: 27.6 us; the launch traced here: 27.4 us
  Pallas kernels  25.2 us (91%)
  local copies, waits for them, and re-layouts  1.56 us (6%)
  between operations  0.64 us (2%)
    pallas_call x1, Pallas kernels, local(): pl.pallas_call(functools.partial(kernel, n, tokens * n), out_shape=(jax.S...  25.2 us
    unnamed x2, local copies, waits for them, and re-layouts  1.56 us

profile of v2, /device:TPU:1, one launch (start us, length us, event | category | flops | bytes accessed | tf_op | source)
XLA Modules:
  0.0 27.4 jit_solution(13296378286977306149)
XLA Ops:
  0.6 25.2 %shard_map.113 = (bf16[8,8,32,256]{3,2,1,0:T(8,128)(2,1)S(1)}, f32[8,16]{1,0:T(8,128)S(1)}) custom-call(bf16[8,8,32,256]{3,2,1,0:T(8,128)(2,1)} %bitcast.5, bf16[8,8,32,256]{3,2,1,0:T(8,128)(2,1)} %bitcast.6, bf16[8,8,32,256]{3,2,1,0:T(8,128)(2,1)} %bitcast.7, f32[8,16]{1,0:T(8,128)} %rate.1, f32[8,16]{1,0:T(8,128)} %resid.1, ...), custom_call_target="tpu_custom_call" | custom-call | tf_op jit(solution)/shard_map/pallas_call | solution.py:368
  25.9 1.0 %copy.14 = bf16[2048,256]{1,0:T(8,128)(2,1)} copy(bf16[2048,256]{1,0:T(8,128)(2,1)S(1)} %bitcast.4) | data formatting | bytes 2097152
  26.8 0.6 %copy.15 = f32[8,16]{1,0:T(8,128)} copy(f32[8,16]{1,0:T(8,128)S(1)} %get-tuple-element.9) | data formatting | bytes 1024

commit v3 on v2

--- a/solution.py
+++ b/solution.py
@@ -338,6 +338,16 @@
     arrived(mgot.at[pl.ds(0, n - 1)], m_send)
     arrived(ugot.at[pl.ds(0, n - 1)], u_send)
     arrived(rgot.at[pl.ds(0, n - 1)], r_send)
+
+
+def store(y, r, out, rgrad, sems):
+    parts = y.shape[0]
+    copies = [pltpu.make_async_copy(r, rgrad, sems.at[parts])]
+    copies += [pltpu.make_async_copy(y.at[j], out.at[j], sems.at[j]) for j in range(parts)]
+    for c in copies:
+        c.start()
+    for c in copies:
+        c.wait()
 
 
 def local(inner, moment, spread, whole, points, gate_value, conv_input, output_grad, decay_rate, residue):
@@ -381,6 +391,13 @@
             decay_rate, residue, inner, moment, spread, whole, points,
         )
     ])
+    out, rgrad = pl.pallas_call(
+        store,
+        out_shape=(jax.ShapeDtypeStruct(cut, bf16), jax.ShapeDtypeStruct(residue.shape, f32)),
+        in_specs=[vmem_spec] * 2,
+        out_specs=(hbm_spec, hbm_spec),
+        scratch_shapes=[dma((CHUNKS + 1,))],
+    )(*[pltpu.with_memory_space_constraint(a, pltpu.VMEM) for a in (out, rgrad)])
     return out.reshape(tokens, channels), rgrad
 
 

time: 27.6 us -> 27 us (0.978)
  local copies, waits for them, and re-layouts: 1.56 us -> 0 us
  Pallas kernels: 25.2 us -> 26.3 us
    unnamed x2 -> x0, local copies, waits for them, and re-layouts: 1.56 us -> none
    pallas_call x0 -> x1, Pallas kernels: none -> 1.04 us  [local(): pl.pallas_call(store, out_shape=(jax.ShapeDtypeStruct(cut, bf16), jax.Sha...]
where the time goes in v3:
time: 27 us; the launch traced here: 26.9 us
  Pallas kernels  26.3 us (97%)
  between operations  0.64 us (2%)
    pallas_call x1, Pallas kernels, local(): pl.pallas_call(functools.partial(kernel, n, tokens * n), out_shape=(jax.S...  25.2 us
    pallas_call x1, Pallas kernels, local(): pl.pallas_call(store, out_shape=(jax.ShapeDtypeStruct(cut, bf16), jax.Sha...  1.04 us

profile of v3, /device:TPU:1, one launch (start us, length us, event | category | flops | bytes accessed | tf_op | source)
XLA Modules:
  0.0 26.9 jit_solution(4542824343981233341)
XLA Ops:
  0.6 25.2 %shard_map.113 = (bf16[8,8,32,256]{3,2,1,0:T(8,128)(2,1)S(1)}, f32[8,16]{1,0:T(8,128)S(1)}) custom-call(bf16[8,8,32,256]{3,2,1,0:T(8,128)(2,1)} %bitcast.4, bf16[8,8,32,256]{3,2,1,0:T(8,128)(2,1)} %bitcast.5, bf16[8,8,32,256]{3,2,1,0:T(8,128)(2,1)} %bitcast.6, f32[8,16]{1,0:T(8,128)} %rate.1, f32[8,16]{1,0:T(8,128)} %resid.1, ...), custom_call_target="tpu_custom_call" | custom-call | tf_op jit(solution)/shard_map/pallas_call | solution.py:378
  25.9 1.0 %shard_map.114 = (bf16[8,8,32,256]{3,2,1,0:T(8,128)(2,1)}, f32[8,16]{1,0:T(8,128)}) custom-call(bf16[8,8,32,256]{3,2,1,0:T(8,128)(2,1)S(1)} %get-tuple-element.6.y, f32[8,16]{1,0:T(8,128)S(1)} %get-tuple-element.7.r), custom_call_target="tpu_custom_call" | custom-call | tf_op jit(solution)/shard_map/pallas_call | solution.py:394

commit v4 on v3

--- a/solution.py
+++ b/solution.py
@@ -77,11 +77,11 @@
     chunk = WIDTH * steps
     span = chunk * CHUNKS
 
+    order = sorted(range(1, n), key=lambda i: -(min(i // 2 % 8, 8 - i // 2 % 8) + i // 16))
+
     def others(body):
-        def step(i, carry):
+        for i in order:
             body(lax.rem(me + i, n))
-            return carry
-        lax.fori_loop(1, n, step, 0)
 
     def put(src, dst, send, recv, e):
         pltpu.make_async_remote_copy(src, dst, send, recv, device_id={"ctx": e}, device_id_type=MESH).start()
@@ -208,13 +208,13 @@
     others(lambda e: put(ubuf.at[e], ugot.at[me], u_send, u_recv, e))
 
     arrived(rates.at[pl.ds(0, n - 1)], rates_recv)
-    tiles = []
-    for e in range(n):
-        a = pltpu.roll(jnp.broadcast_to(rates[e, 0:1], (8, 128)), 0, 1, stride=16, stride_axis=0)
-        b = pltpu.roll(jnp.broadcast_to(rates[e, 1:2], (8, 128)), 16, 1, stride=16, stride_axis=0)
-        tiles.append(jnp.where(lane < 16, a, b))
-    turned = jnp.concatenate(tiles, axis=0).T
-    lam, res = turned[0:16], turned[16:32]
+    def to_modes(row_of):
+        tiles = [
+            pltpu.roll(jnp.broadcast_to(row_of(e), (8, 128)), 0, 1, stride=16, stride_axis=0) for e in range(n)
+        ]
+        return jnp.concatenate(tiles, axis=0).T[0:16]
+
+    lam = to_modes(lambda e: rates[e, 0:1])
     lam_s[...] = lam
     lamh_s[0:16] = lam[:, 0:128]
     lamh_s[16:32] = lam[:, 128:256]
@@ -234,8 +234,6 @@
         b = behind * term
         en[k] = e
         fx[k] = b
-        fo[k] = b * res
-        tau[k] = jnp.sum(e * res, axis=0, keepdims=True)
         power = power * h
 
     def scan(r, carry):
@@ -293,6 +291,11 @@
     rgot[me] = rbuf[me]
     others(lambda e: put(rbuf.at[e], rgot.at[me], r_send, r_recv, e))
 
+    res = to_modes(lambda e: rates[e, 1:2])
+    for k in range(TERMS):
+        fo[k] = fx[k] * res
+        tau[k] = jnp.sum(en[k] * res, axis=0, keepdims=True)
+
     def within(q, carry):
         s = s_v[q]
         acc = tau[0] * jnp.dot(inner_v[0], s, preferred_element_type=f32)
@@ -301,14 +304,11 @@
         yin[q] = acc
         return carry
 
-    lax.fori_loop(0, steps, within, 0)
+    lax.fori_loop(0, steps, within, 0, unroll=2)
     tabs[4].wait()
 
     arrived(ugot.at[pl.ds(0, n - 1)], u_recv)
-    tiles = [
-        pltpu.roll(jnp.broadcast_to(ugot[e], (8, 128)), 0, 1, stride=16, stride_axis=0) for e in range(n)
-    ]
-    turned = jnp.concatenate(tiles, axis=0).T
+    turned = to_modes(lambda e: ugot[e])
     for r in range(16):
         st[r] = cin[r] + p256[r] * turned[r : r + 1]
 

time: 27 us -> 26 us (0.963)
  Pallas kernels: 26.3 us -> 25.3 us
    pallas_call x1, Pallas kernels: 25.2 us -> 24.2 us  [local(): pl.pallas_call(functools.partial(kernel, n, tokens * n), out_shape=(jax.S...]
where the time goes in v4:
time: 26 us; the launch traced here: 25.9 us
  Pallas kernels  25.3 us (97%)
  between operations  0.64 us (2%)
    pallas_call x1, Pallas kernels, local(): pl.pallas_call(functools.partial(kernel, n, tokens * n), out_shape=(jax.S...  24.2 us
    pallas_call x1, Pallas kernels, local(): pl.pallas_call(store, out_shape=(jax.ShapeDtypeStruct(cut, bf16), jax.Sha...  1.04 us

profile of v4, /device:TPU:1, one launch (start us, length us, event | category | flops | bytes accessed | tf_op | source)
XLA Modules:
  0.0 25.9 jit_solution(11421047900044284066)
XLA Ops:
  0.6 24.2 %shard_map.113 = (bf16[8,8,32,256]{3,2,1,0:T(8,128)(2,1)S(1)}, f32[8,16]{1,0:T(8,128)S(1)}) custom-call(bf16[8,8,32,256]{3,2,1,0:T(8,128)(2,1)} %bitcast.4, bf16[8,8,32,256]{3,2,1,0:T(8,128)(2,1)} %bitcast.5, bf16[8,8,32,256]{3,2,1,0:T(8,128)(2,1)} %bitcast.6, f32[8,16]{1,0:T(8,128)} %rate.1, f32[8,16]{1,0:T(8,128)} %resid.1, ...), custom_call_target="tpu_custom_call" | custom-call | tf_op jit(solution)/shard_map/pallas_call | solution.py:378
  24.9 1.0 %shard_map.114 = (bf16[8,8,32,256]{3,2,1,0:T(8,128)(2,1)}, f32[8,16]{1,0:T(8,128)}) custom-call(bf16[8,8,32,256]{3,2,1,0:T(8,128)(2,1)S(1)} %get-tuple-element.6.y, f32[8,16]{1,0:T(8,128)S(1)} %get-tuple-element.7.r), custom_call_target="tpu_custom_call" | custom-call | tf_op jit(solution)/shard_map/pallas_call | solution.py:394
